TPU v7x, 256 devices: a whole 4x4x8 slice. The times are simulated.
256 devices in a mesh: exp: 128 (over x, z, y), dp: 2 (over core).
Axes of the slice: x: 4, y: 4, z: 8, core: 2. Of those that a mesh axis runs over, the one named last changes fastest.
Arguments:
- grad_out: bfloat16 [32768, 2880], P(('exp', 'dp')), may hold values from -6 to 6
- combine: float32 [32768, 4], P(('exp', 'dp')), may hold values from 0.05 to 0.6
- routes: int32 [32768, 4], P(('exp', 'dp')), may hold values from 0 to 127, as said below
- tasks: int32 [32768], P(('exp', 'dp')), may hold values from 0 to 3, as said below
- task_lists: int32 [4, 64], replicated, may hold values from 0 to 127, as said below
- gate_up: bfloat16 [128, 1536, 2880], P('exp', 'dp'), may hold values from -6 to 6
Outputs:
- grad_down: bfloat16 [128, 1440, 2880], P('exp', 'dp')
Inputs may be any that keep to these rules, and one draw needn't show every extreme that they name: `routes`: in the 128 tokens of one device no expert is named more than 6 times, and some expert is named exactly 6 times; each token names 4 different experts. `tasks`: all 128 tokens of one device belong to one task. `task_lists`: each row names 64 different experts.
All inputs are finite; a program needn't handle non-finite values.
Results may differ from a plain program's by a relative error of at most 0.0057.
Values may be sent and summed in bfloat16 or wider, within the bound.
A program may use at most 128 MiB of HBM per device.

v0:
```python
import jax
import jax.numpy as jnp
from jax import lax
from jax.sharding import PartitionSpec as P


def expert_hidden(gate_up):
    half_width = gate_up.shape[-1] // 2
    gate_pre = gate_up[..., :half_width].astype(jnp.float32)
    up_pre = gate_up[..., half_width:].astype(jnp.float32)
    return ((up_pre + 1.0) * gate_pre * jax.nn.sigmoid(1.702 * gate_pre)).astype(jnp.bfloat16)


def outer_rows(left_rows, right_rows):
    return lax.dot_general(
        left_rows, right_rows, (((0,), (0,)), ((), ())), preferred_element_type=jnp.float32
    )


def body(grad_out, combine, routes, tasks, task_lists, gate_up):
    n_experts = lax.axis_size("exp")
    slot_rows = gate_up.shape[1]
    capacity = slot_rows // n_experts
    model_width = grad_out.shape[1]
    tok_count = routes.shape[0]
    top_count = routes.shape[1]
    task_count = task_lists.shape[0]
    expert_ids = lax.iota(jnp.int32, n_experts)
    member = jnp.any(task_lists[:, :, None] == expert_ids[None, None, :], axis=1).astype(
        jnp.float32
    )
    task_onehot = (tasks[:, None] == lax.iota(jnp.int32, task_count)[None, :]).astype(jnp.float32)
    token_member = jnp.dot(task_onehot, member) > 0.5
    route_onehot = (routes[:, :, None] == expert_ids[None, None, :]).astype(jnp.int32)
    keep_flags = jnp.sum(route_onehot * token_member[:, None, :].astype(jnp.int32), axis=2)
    flat_onehot = route_onehot.reshape(tok_count * top_count, n_experts)
    running = jnp.cumsum(flat_onehot, axis=0) - 1
    slot_index = jnp.sum(flat_onehot * running, axis=1)
    destination = routes.reshape(-1) * capacity + slot_index
    routed = (combine[:, :, None] * grad_out[:, None, :].astype(jnp.float32)).astype(jnp.bfloat16)
    routed = routed.reshape(tok_count * top_count, model_width)
    send_rows = (
        jnp.zeros((n_experts * capacity, model_width), jnp.bfloat16).at[destination].set(routed)
    )
    send_keep = (
        jnp.zeros((n_experts * capacity,), jnp.bfloat16)
        .at[destination]
        .set(keep_flags.reshape(-1).astype(jnp.bfloat16))
    )
    recv_rows, recv_keep = (
        lax.all_to_all(send_rows, "exp", split_axis=0, concat_axis=0, tiled=True),
        lax.all_to_all(send_keep, "exp", split_axis=0, concat_axis=0, tiled=True),
    )
    masked = jnp.where(recv_keep[:, None] > 0, recv_rows, jnp.zeros_like(recv_rows))
    hidden = expert_hidden(gate_up[0])
    summed = lax.psum_scatter(outer_rows(hidden, masked), "dp", scatter_dimension=0, tiled=True)
    return summed.astype(jnp.bfloat16)[None]


def solution(mesh):
    in_specs = (
        P(("exp", "dp"), None),
        P(("exp", "dp"), None),
        P(("exp", "dp"), None),
        P(("exp", "dp")),
        P(),
        P("exp", "dp", None),
    )
    out_specs = P("exp", "dp", None)
    return jax.shard_map(body, mesh=mesh, in_specs=in_specs, out_specs=out_specs, check_vma=False)
```

profile of v0, /device:TPU:1, one launch (start us, length us, event | category | flops | bytes accessed | tf_op | source)
XLA Modules:
  0.0 278.3 jit_solution(11325586234444520709)
XLA Ops:
  6.5 0.7 broadcast_multiply_fusion
  7.2 0.8 copy.27
  8.2 0.8 fusion.23
  9.2 0.9 fusion.18
  10.1 0.9 select_reduce_fusion
  11.4 0.2 fusion.20
  11.8 0.2 fusion.19
  12.0 3.8 %scatter_custom_fusion = bf16[768]{0:T(1024)(128)(2,1)S(1)} fusion(s32[512]{0:T(512)S(1)} %bitcast.17, bf16[512]{0:T(512)(128)(2,1)S(1)} %reshape.79, bf16[]{:T(256)} %constant.11.clone.1), kind=kCustom, calls=%fused_computation.43 | custom fusion | bytes 1538 | tf_op jit(solution)/shard_map/scatter | solution.py:48
  15.8 0.8 all_to_all.19
  16.6 16.5 %all-to-all-start = ((bf16[128,6,1]{1,2,0:T(2,128)(2,1)}), bf16[128,6,1]{1,2,0:T(2,128)(2,1)S(1)}, u32[]{:S(2)}, u32[]{:S(2)}) async-start(bf16[128,6,1]{1,2,0:T(2,128)(2,1)} %all_to_all.19), calls=%async_computation | async-start | bytes 131072 | tf_op jit(solution)/shard_map/all_to_all | solution.py:52
  33.1 0.8 copy.33
  34.0 1.4 copy.34
  35.4 3.6 %mul.69 = f32[128,4,2880]{2,1,0:T(4,128)} broadcast(f32[128,2880]{1,0:T(8,128)S(1)} %copy.34), dimensions={0,2} | broadcast | bytes 7372800 | tf_op jit(solution)/shard_map/mul | solution.py:40
  39.0 7.8 %mul.70 = f32[512,2880]{1,0:T(8,128)} reshape(f32[128,4,2880]{2,1,0:T(4,128)} %mul.69) | data formatting | bytes 11796480 | tf_op jit(solution)/shard_map/mul | solution.py:40
  46.8 9.6 %scatter_custom_fusion.1 = bf16[768,2880]{1,0:T(8,128)(2,1)} fusion(s32[512]{0:T(512)S(1)} %bitcast.18, f32[512,2880]{1,0:T(8,128)} %mul.70, f32[512]{0:T(512)S(1)} %mul.67, bf16[]{:T(256)} %constant.11.clone.1), kind=kCustom, calls=%fused_computation.15 | custom fusion | flops 2949120 | bytes 10323970 | tf_op jit(solution)/shard_map/scatter | solution.py:43
  56.5 7.6 %all_to_all.16 = bf16[128,6,2880]{2,1,0:T(8,128)(2,1)} reshape(bf16[768,2880]{1,0:T(8,128)(2,1)} %scatter_custom_fusion.1) | data formatting | bytes 8847360 | tf_op jit(solution)/shard_map/all_to_all | solution.py:51
  64.1 13.5 %all-to-all-start.1 = ((bf16[128,6,2880]{2,1,0:T(8,128)(2,1)}), bf16[128,6,2880]{2,1,0:T(8,128)(2,1)}, u32[]{:S(2)}, u32[]{:S(2)}) async-start(bf16[128,6,2880]{2,1,0:T(8,128)(2,1)} %all_to_all.16), calls=%async_computation.1 | async-start | bytes 12058624 | tf_op jit(solution)/shard_map/all_to_all | solution.py:51
  77.6 0.3 reduce-scatter.2.cloned.1.call-start
  77.9 0.2 compare_reduce_fusion
  78.2 130.4 %all-to-all-done.1 = bf16[128,6,2880]{2,1,0:T(8,128)(2,1)} async-done(((bf16[128,6,2880]{2,1,0:T(8,128)(2,1)}), bf16[128,6,2880]{2,1,0:T(8,128)(2,1)}, u32[]{:S(2)}, u32[]{:S(2)}) %all-to-all-start.1) | async-done | bytes 4423712 | tf_op jit(solution)/shard_map/all_to_all | solution.py:51
  208.6 8.2 %all_to_all.18 = bf16[768,2880]{1,0:T(8,128)(2,1)} reshape(bf16[128,6,2880]{2,1,0:T(8,128)(2,1)} %all-to-all-done.1) | data formatting | bytes 8847360 | tf_op jit(solution)/shard_map/all_to_all | solution.py:51
  216.8 14.4 %fusion = f32[1440,2880]{1,0:T(8,128)} fusion(bf16[768,2880]{1,0:T(8,128)(2,1)} %all_to_all.18, pred[768]{0:T(1024)(128)(4,1)S(1)} %gt.21, bf16[768,2880]{0,1:T(8,128)(2,1)} %bitcast.19), kind=kOutput, calls=%fused_computation.5 | convolution fusion | flops 6383370240 | bytes 25436928 | tf_op jit(solution)/shard_map/dot_general | solution.py:15
  231.2 34.4 %reduce-scatter.2.cloned.1.call-done = f32[720,2880]{1,0:T(8,128)} async-done(((f32[1440,2880]{1,0:T(8,128)}), f32[720,2880]{1,0:T(8,128)}) %reduce-scatter.2.cloned.1.call-update) | async-done | bytes 8294416 | tf_op jit(solution)/shard_map/reduce_scatter | solution.py:56
  265.6 5.9 %convert_bitcast_fusion = bf16[1,720,2880]{2,1,0:T(8,128)(2,1)} fusion(f32[720,2880]{1,0:T(8,128)} %reduce-scatter.2.cloned.1.call-done), kind=kLoop, calls=%fused_computation.14 | loop fusion | flops 2073600 | bytes 12441600 | tf_op jit(solution)/shard_map/broadcast_in_dim | solution.py:57
  (18 shorter events, 1.2 us)
Async XLA Ops:
  16.6 47.5 %all-to-all-start = ((bf16[128,6,1]{1,2,0:T(2,128)(2,1)}), bf16[128,6,1]{1,2,0:T(2,128)(2,1)S(1)}, u32[]{:S(2)}, u32[]{:S(2)}) async-start(bf16[128,6,1]{1,2,0:T(2,128)(2,1)} %all_to_all.19), calls=%async_computation | async-start | bytes 131072 | tf_op jit(solution)/shard_map/all_to_all | solution.py:52
  64.1 144.6 %all-to-all-start.1 = ((bf16[128,6,2880]{2,1,0:T(8,128)(2,1)}), bf16[128,6,2880]{2,1,0:T(8,128)(2,1)}, u32[]{:S(2)}, u32[]{:S(2)}) async-start(bf16[128,6,2880]{2,1,0:T(8,128)(2,1)} %all_to_all.16), calls=%async_computation.1 | async-start | bytes 12058624 | tf_op jit(solution)/shard_map/all_to_all | solution.py:51
  77.6 188.0 %reduce-scatter.2.cloned.1.call-start = ((), (), s32[]{:S(2)}) async-start(), calls=%async_computation.3 | async-start | bytes 25436160 | tf_op jit(solution)/shard_map/reduce_scatter | solution.py:56
Sparse Core Ops, SparseCore 0:
  231.4 34.1 reduce-scatter.1
where the time goes:
time: 279 us; the launch traced here: 278 us
  waiting for transfers between devices  165 us (59%)
  local copies, waits for them, and re-layouts  35.8 us (13%)
  starting transfers between devices  30.3 us (11%)
  other arithmetic  18.7 us (7%)
  matrix products  15.2 us (5%)
  between operations  13.5 us (5%)
    all_to_all x1, waiting for transfers between devices, body(): lax.all_to_all(send_rows, 'exp', split_axis=0, concat_axis=0, tiled=True)  130 us
    reduce_scatter x1, waiting for transfers between devices, body(): lax.psum_scatter(outer_rows(hidden, masked), 'dp', scatter_dimension=0, t...  34.4 us
    all_to_all x1, starting transfers between devices, body(): lax.all_to_all(send_keep, 'exp', split_axis=0, concat_axis=0, tiled=True)  16.5 us
    all_to_all x2, local copies, waits for them, and re-layouts, body(): lax.all_to_all(send_rows, 'exp', split_axis=0, concat_axis=0, tiled=True)  15.8 us
    dot_general x1, matrix products, outer_rows(): lax.dot_general(left_rows, right_rows, (((0,), (0,)), ((), ())), preferre...  14.4 us
    all_to_all x1, starting transfers between devices, body(): lax.all_to_all(send_rows, 'exp', split_axis=0, concat_axis=0, tiled=True)  13.5 us
    mul x3, local copies, waits for them, and re-layouts, body(): combine[:, :, None] * grad_out[:, None, :].astype(jnp.float32)  11.5 us
    scatter x1, other arithmetic, body(): jnp.zeros((n_experts * capacity, model_width), jnp.bfloat16).at[destination]  9.63 us
  transfers between devices with their start and end apart: 3, of which 2 were waited for; matrix products, arithmetic and copies ran while one was open for 9% of the time, Pallas kernels for 0%

commit v1 on v0

--- a/solution.py
+++ b/solution.py
@@ -1,7 +1,17 @@
+import functools
+
 import jax
 import jax.numpy as jnp
 from jax import lax
+from jax.experimental import pallas as pl
+from jax.experimental.pallas import tpu as pltpu
 from jax.sharding import PartitionSpec as P
+
+F32, BF16, I32 = jnp.float32, jnp.bfloat16, jnp.int32
+MESH = pl.DeviceIdType.MESH
+GRID = {128: (4, 8, 4), 8: (2, 2, 2)}
+CAPACITY = {128: 80, 8: 16}
+CHUNK = {2880: 512, 320: 128}
 
 
 def expert_hidden(gate_up):
@@ -17,7 +27,7 @@
     )
 
 
-def body(grad_out, combine, routes, tasks, task_lists, gate_up):
+def dense_body(grad_out, combine, routes, tasks, task_lists, gate_up):
     n_experts = lax.axis_size("exp")
     slot_rows = gate_up.shape[1]
     capacity = slot_rows // n_experts
@@ -54,7 +64,394 @@
     masked = jnp.where(recv_keep[:, None] > 0, recv_rows, jnp.zeros_like(recv_rows))
     hidden = expert_hidden(gate_up[0])
     summed = lax.psum_scatter(outer_rows(hidden, masked), "dp", scatter_dimension=0, tiled=True)
-    return summed.astype(jnp.bfloat16)[None]
+    return summed.astype(jnp.bfloat16)
+
+
+def iota(shape, dim):
+    return lax.broadcasted_iota(I32, shape, dim)
+
+
+def whole_part(values, step):
+    return jnp.floor((values.astype(F32) + 0.5) * (1.0 / step)).astype(I32)
+
+
+def dot(left, right):
+    return jnp.dot(left, right, preferred_element_type=F32)
+
+
+def dot_lanes(left, right):
+    return lax.dot_general(left, right, (((1,), (1,)), ((), ())), preferred_element_type=F32)
+
+
+def tiles_of(width, step):
+    return [(start, min(step, width - start)) for start in range(0, width, step)]
+
+
+def kernel(
+    sizes, tok_ref, comb_ref, routes_ref, task_ref, lists_ref, gate_up_ref,
+    out_ref, flag_ref, *scratch,
+):
+    (nx, nz, ny), cap, cap_rows, room, chunks = sizes
+    n_chunks = len(chunks)
+    width, tok_count = tok_ref.shape
+    double, slot_rows = gate_up_ref.shape
+    hidden_width = double // 2
+    half = hidden_width // 2
+    experts, plane = nx * nz * ny, nx * ny
+    block = nz * cap
+
+    scratch = list(scratch)
+    take = lambda count: [scratch.pop(0) for _ in range(count)]
+    z_send, z_recv, xy_send, xy_recv = (take(n_chunks) for _ in range(4))
+    own, dp_send, dp_recv, out_buf = (take(n_chunks) for _ in range(4))
+    pick, gu, hidden, spread, weight = take(5)
+    meta_send, meta_recv, note_send, note_recv, last_send, last_recv = take(6)
+    zs_sem, zr_sem, xs_sem, xr_sem, ds_sem, dr_sem, out_sem = take(7)
+    ms_sem, mr_sem, ns_sem, nr_sem, ls_sem, lr_sem, gu_sem = take(7)
+    zl_sem, xl_sem, ml_sem, nl_sem = take(4)
+
+    e_id, p = lax.axis_index("exp"), lax.axis_index("dp")
+    y = lax.rem(e_id, ny)
+    z = lax.rem(lax.div(e_id, ny), nz)
+    x = lax.div(e_id, ny * nz)
+    q = x * ny + y
+    z_steps = sorted(range(1, nz), key=lambda d: -min(d, nz - d))
+    xy_steps = sorted(
+        ((dx, dy) for dx in range(nx) for dy in range(ny) if dx or dy),
+        key=lambda s: -(min(s[0], nx - s[0]) + min(s[1], ny - s[1])),
+    )
+
+    def z_at(z2):
+        return ((x * nz + z2) * ny + y, p)
+
+    def xy_at(x2, y2):
+        return ((x2 * nz + z) * ny + y2, p)
+
+    sibling = (e_id, 1 - p)
+
+    gu_copy = pltpu.make_async_copy(gate_up_ref, gu, gu_sem)
+    gu_copy.start()
+
+    barrier = pltpu.get_barrier_semaphore()
+    for d in z_steps:
+        pl.semaphore_signal(barrier, inc=1, device_id=z_at(lax.rem(z + d, nz)), device_id_type=MESH)
+    for dx, dy in xy_steps:
+        pl.semaphore_signal(
+            barrier, inc=1, device_id=xy_at(lax.rem(x + dx, nx), lax.rem(y + dy, ny)),
+            device_id_type=MESH,
+        )
+    pl.semaphore_signal(barrier, inc=1, device_id=sibling, device_id_type=MESH)
+
+    expert_col = iota((experts, tok_count), 0)
+    named = jnp.zeros((experts, tok_count), F32)
+    weight_of = jnp.zeros((experts, tok_count), F32)
+    for k in range(routes_ref.shape[0]):
+        hit = expert_col == routes_ref[k : k + 1, :]
+        named = jnp.where(hit, 1.0, named)
+        weight_of = jnp.where(hit, comb_ref[k : k + 1, :], weight_of)
+    lists = lists_ref[...]
+    of_task = iota(lists.shape, 0) == task_ref[0:1, 0:1]
+    chosen = jnp.max(jnp.where(of_task, lists, -1), axis=0, keepdims=True)
+    trainable = jnp.max(
+        jnp.where(iota((experts, lists.shape[1]), 0) == chosen, 1.0, 0.0), axis=1, keepdims=True
+    )
+    before = jnp.where(
+        iota((tok_count, tok_count), 0) < iota((tok_count, tok_count), 1), 1.0, 0.0
+    ).astype(BF16)
+    slot = dot(named.astype(BF16), before)
+    live = named * trainable
+    expert_plane = lax.rem(lax.shift_right_logical(iota((nz, experts), 1), ny.bit_length() - 1), nz)
+    in_plane = jnp.where(expert_plane == iota((nz, experts), 0), 1.0, 0.0).astype(BF16)
+    wanted = dot(in_plane, live.astype(BF16)) > 0.5
+    place = dot(jnp.where(wanted, 1.0, 0.0).astype(BF16), before)
+    over = jnp.max(jnp.where(wanted & (place > room - 0.5), 1.0, 0.0), axis=1, keepdims=True)
+    over = jnp.max(over, axis=0, keepdims=True)
+    place = jnp.where(wanted, place, -1.0)
+    row_id = iota((room, tok_count), 0).astype(F32)
+    for z2 in range(nz):
+        pick[z2 * room : (z2 + 1) * room, :] = jnp.where(
+            row_id == place[z2 : z2 + 1, :], 1.0, 0.0
+        ).astype(BF16)
+
+    def send_z(j):
+        start, size = chunks[j]
+        z_send[j][...] = (
+            dot_lanes(pick[...], tok_ref[start : start + size, :])
+            .astype(BF16)
+            .reshape(z_send[j].shape)
+        )
+        for d in z_steps:
+            z2 = lax.rem(z + d, nz)
+            z_copy(j, z2).start()
+        pltpu.make_async_copy(z_send[j].at[z], z_recv[j].at[z], zl_sem.at[j]).start()
+
+    def z_copy(j, z2):
+        return pltpu.make_async_remote_copy(
+            src_ref=z_send[j].at[z2], dst_ref=z_recv[j].at[z],
+            send_sem=zs_sem.at[j, z2], recv_sem=zr_sem.at[j, z],
+            device_id=z_at(z2), device_id_type=MESH,
+        )
+
+    def meta_copy(z2):
+        return pltpu.make_async_remote_copy(
+            src_ref=meta_send, dst_ref=meta_recv.at[z],
+            send_sem=ms_sem.at[z2], recv_sem=mr_sem.at[z],
+            device_id=z_at(z2), device_id_type=MESH,
+        )
+
+    def wait_from(ref, sem, device):
+        pltpu.make_async_remote_copy(
+            src_ref=ref, dst_ref=ref, send_sem=sem, recv_sem=sem,
+            device_id=device, device_id_type=MESH,
+        ).wait_recv()
+
+    pl.semaphore_wait(barrier, len(z_steps) + len(xy_steps) + 1)
+    send_z(0)
+
+    place_of = lax.dot_general(
+        in_plane, place.astype(BF16), (((0,), (0,)), ((), ())), preferred_element_type=F32
+    )
+    meta_lane = iota((experts, 128), 1)
+    meta = jnp.zeros((experts, 128), F32)
+    for c in range(cap):
+        here = jnp.where((slot > c - 0.5) & (slot < c + 0.5), live, 0.0)
+        at = jnp.sum(here * (place_of + 1.0), axis=1, keepdims=True)
+        w = jnp.sum(here * weight_of, axis=1, keepdims=True)
+        high = w.astype(BF16).astype(F32)
+        mid = (w - high).astype(BF16).astype(F32)
+        for kind, value in enumerate((at, high, mid, w - high - mid)):
+            meta = jnp.where(meta_lane == kind * cap_rows + c, value, meta)
+    meta = jnp.where(meta_lane == cap, over, meta)
+    meta_send[...] = jnp.transpose(meta)[: 4 * cap_rows, :].astype(BF16)
+    for d in z_steps:
+        meta_copy(lax.rem(z + d, nz)).start()
+    pltpu.make_async_copy(meta_send, meta_recv.at[z], ml_sem).start()
+    if n_chunks > 1:
+        send_z(1)
+
+    gu_copy.wait()
+    step = 96 if hidden_width % 96 == 0 else 32
+
+    @pl.loop(0, hidden_width // step)
+    def _(i):
+        rows = pl.ds(pl.multiple_of(i * step, step), step)
+        gate = gu[rows, :].astype(F32)
+        up = gu[pl.ds(pl.multiple_of(i * step + hidden_width, step), step), :].astype(F32)
+        gu[rows, :] = ((up + 1.0) * gate * jax.nn.sigmoid(1.702 * gate)).astype(BF16)
+
+    for start, size in tiles_of(slot_rows, 256):
+        to = iota((slot_rows, size), 1) + start
+        to_q = whole_part(to, block)
+        rest = to - to_q * block
+        to_z = whole_part(rest, cap)
+        c = rest - to_z * cap
+        to_x = whole_part(to_q, ny)
+        source = ((to_x * nz + to_z) * ny + (to_q - to_x * ny)) * cap + c
+        order = jnp.where(iota((slot_rows, size), 0) == source, 1.0, 0.0).astype(BF16)
+        hidden[:, start : start + size] = dot(gu[0:hidden_width, :], order).astype(BF16)
+
+    for d in z_steps:
+        z2 = lax.rem(z + nz - d, nz)
+        wait_from(meta_recv.at[z2], mr_sem.at[z2], z_at(z2))
+    pltpu.make_async_copy(meta_send, meta_recv.at[z], ml_sem).wait()
+    s_col = iota((slot_rows, experts), 0)
+    s_q = whole_part(s_col, block)
+    s_x = whole_part(s_q, ny)
+    expert_of = (s_x * nz + z) * ny + (s_q - s_x * ny)
+    at_expert = jnp.where(expert_of == iota((slot_rows, experts), 1), 1.0, 0.0).astype(BF16)
+    m_col = iota((slot_rows, cap_rows * 4), 0)
+    m_lane = iota((slot_rows, cap_rows * 4), 1)
+    m_rest = m_col - whole_part(m_col, block) * block
+    m_z = whole_part(m_rest, cap)
+    m_c = m_rest - m_z * cap
+    totals = jnp.zeros((slot_rows, cap_rows * 4), F32)
+    noted = jnp.zeros((1, experts), F32)
+    for z2 in range(nz):
+        table = meta_recv[z2]
+        noted = jnp.maximum(noted, table[cap : cap + 1, :].astype(F32))
+        found = dot_lanes(at_expert, table)
+        totals = jnp.where(m_z == z2, found, totals)
+    kind_of = whole_part(m_lane, cap_rows)
+    slot_hit = m_lane - kind_of * cap_rows == m_c
+    at = jnp.sum(jnp.where(slot_hit & (kind_of == 0), totals, 0.0), axis=1, keepdims=True)
+    w = jnp.sum(jnp.where(slot_hit & (kind_of > 0), totals, 0.0), axis=1, keepdims=True)
+    weight[...] = jnp.broadcast_to(w, weight.shape)
+    r_col = iota((slot_rows, 1), 0)
+    r_rest = r_col - whole_part(r_col, block) * block
+    at = jnp.where(at > 0.5, at - 1.0 + (whole_part(r_rest, cap) * room).astype(F32), -1.0)
+    spread[...] = jnp.where(
+        iota((slot_rows, nz * room), 1).astype(F32) == at, 1.0, 0.0
+    ).astype(BF16)
+    note_send[...] = jnp.broadcast_to(
+        jnp.max(noted, axis=1, keepdims=True), note_send.shape
+    ).astype(BF16)
+
+    def note_copy(x2, y2):
+        q2 = x2 * ny + y2
+        return pltpu.make_async_remote_copy(
+            src_ref=note_send, dst_ref=note_recv.at[q],
+            send_sem=ns_sem.at[q2], recv_sem=nr_sem.at[q],
+            device_id=xy_at(x2, y2), device_id_type=MESH,
+        )
+
+    def xy_copy(j, x2, y2):
+        q2 = x2 * ny + y2
+        return pltpu.make_async_remote_copy(
+            src_ref=xy_send[j].at[q2], dst_ref=xy_recv[j].at[q],
+            send_sem=xs_sem.at[j, q2], recv_sem=xr_sem.at[j, q],
+            device_id=xy_at(x2, y2), device_id_type=MESH,
+        )
+
+    def dp_copy(j):
+        return pltpu.make_async_remote_copy(
+            src_ref=dp_send[j], dst_ref=dp_recv[j], send_sem=ds_sem.at[j], recv_sem=dr_sem.at[j],
+            device_id=sibling, device_id_type=MESH,
+        )
+
+    def each_xy(act):
+        for dx, dy in xy_steps:
+            act(lax.rem(x + dx, nx), lax.rem(y + dy, ny))
+
+    def send_xy(j):
+        for d in z_steps:
+            z2 = lax.rem(z + nz - d, nz)
+            wait_from(z_recv[j].at[z2], zr_sem.at[j, z2], z_at(z2))
+        pltpu.make_async_copy(z_send[j].at[z], z_recv[j].at[z], zl_sem.at[j]).wait()
+        if j + 2 < n_chunks:
+            send_z(j + 2)
+        size = chunks[j][1]
+        for start, part in tiles_of(size, 256):
+            rows = z_recv[j][:, :, start : start + part].reshape(nz * room, part)
+            found = dot(spread[...], rows)
+            by = jnp.concatenate([weight[...]] * 2, axis=1)[:, :part]
+            xy_send[j][:, :, start : start + part] = (found * by).astype(BF16).reshape(
+                plane, block, part
+            )
+        each_xy(lambda x2, y2: xy_copy(j, x2, y2).start())
+        pltpu.make_async_copy(xy_send[j].at[q], xy_recv[j].at[q], xl_sem.at[j]).start()
+
+    def multiply(j):
+        def arrived(x2, y2):
+            q2 = x2 * ny + y2
+            wait_from(xy_recv[j].at[q2], xr_sem.at[j, q2], xy_at(x2, y2))
+
+        each_xy(arrived)
+        pltpu.make_async_copy(xy_send[j].at[q], xy_recv[j].at[q], xl_sem.at[j]).wait()
+        theirs = pl.ds(pl.multiple_of((1 - p) * half, 16), half)
+        mine = pl.ds(pl.multiple_of(p * half, 16), half)
+        size = chunks[j][1]
+        for start, part in tiles_of(size, 256):
+            rows = xy_recv[j][:, :, start : start + part].reshape(slot_rows, part)
+            dp_send[j][:, start : start + part] = dot(hidden[theirs, :], rows).astype(BF16)
+        dp_copy(j).start()
+        for start, part in tiles_of(size, 256):
+            rows = xy_recv[j][:, :, start : start + part].reshape(slot_rows, part)
+            own[j][:, start : start + part] = dot(hidden[mine, :], rows)
+
+    def out_copy(j):
+        start, size = chunks[j]
+        return pltpu.make_async_copy(
+            out_buf[j], out_ref.at[:, start : start + size], out_sem.at[j]
+        )
+
+    def finish(j):
+        dp_copy(j).wait_recv()
+        out_buf[j][...] = (own[j][...] + dp_recv[j][...].astype(F32)).astype(BF16)
+        out_copy(j).start()
+
+    each_xy(lambda x2, y2: note_copy(x2, y2).start())
+    pltpu.make_async_copy(note_send, note_recv.at[q], nl_sem).start()
+    for j in range(n_chunks + 2):
+        if j < n_chunks:
+            send_xy(j)
+        if 1 <= j <= n_chunks:
+            multiply(j - 1)
+        if j == n_chunks - 1:
+            def told(x2, y2):
+                q2 = x2 * ny + y2
+                wait_from(note_recv.at[q2], nr_sem.at[q2], xy_at(x2, y2))
+
+            each_xy(told)
+            pltpu.make_async_copy(note_send, note_recv.at[q], nl_sem).wait()
+            last_send[...] = jnp.max(note_recv[...].astype(F32), axis=0).astype(BF16)
+            last = pltpu.make_async_remote_copy(
+                src_ref=last_send, dst_ref=last_recv, send_sem=ls_sem, recv_sem=lr_sem,
+                device_id=sibling, device_id_type=MESH,
+            )
+            last.start()
+        if 2 <= j:
+            finish(j - 2)
+
+    last.wait()
+    flag_ref[...] = jnp.maximum(last_send[...].astype(F32), last_recv[...].astype(F32))[0:8, :]
+    for d in z_steps:
+        meta_copy(lax.rem(z + d, nz)).wait_send()
+    each_xy(lambda x2, y2: note_copy(x2, y2).wait_send())
+    for j in range(n_chunks):
+        for d in z_steps:
+            z_copy(j, lax.rem(z + d, nz)).wait_send()
+        each_xy(lambda x2, y2: xy_copy(j, x2, y2).wait_send())
+        dp_copy(j).wait_send()
+        out_copy(j).wait()
+
+
+def fast_body(grad_out, combine, routes, tasks, task_lists, gate_up):
+    n_experts = lax.axis_size("exp")
+    nx, nz, ny = GRID[n_experts]
+    slot_rows = gate_up.shape[1]
+    cap = slot_rows // n_experts
+    cap_rows = -(-(cap + 1) // 8) * 8
+    room = CAPACITY[n_experts]
+    tok_count, width = grad_out.shape
+    chunks = tiles_of(width, CHUNK[width])
+    hidden_width = gate_up.shape[2] // 2
+    half = hidden_width // 2
+    plane, block = nx * ny, nz * cap
+    n = len(chunks)
+    dma = pltpu.SemaphoreType.DMA
+    each = lambda shape, kind: [pltpu.VMEM((*shape, size), kind) for _, size in chunks]
+    meta = (4 * cap_rows, n_experts)
+    scratch = (
+        each((nz, room), BF16) + each((nz, room), BF16)
+        + each((plane, block), BF16) + each((plane, block), BF16)
+        + each((half,), F32) + each((half,), BF16) + each((half,), BF16) + each((half,), BF16)
+        + [
+            pltpu.VMEM((nz * room, tok_count), BF16),
+            pltpu.VMEM((2 * hidden_width, slot_rows), BF16),
+            pltpu.VMEM((hidden_width, slot_rows), BF16),
+            pltpu.VMEM((slot_rows, nz * room), BF16),
+            pltpu.VMEM((slot_rows, 128), F32),
+            pltpu.VMEM(meta, BF16), pltpu.VMEM((nz, *meta), BF16),
+            pltpu.VMEM((16, 128), BF16), pltpu.VMEM((plane, 16, 128), BF16),
+            pltpu.VMEM((16, 128), BF16), pltpu.VMEM((16, 128), BF16),
+            dma((n, nz)), dma((n, nz)), dma((n, plane)), dma((n, plane)),
+            dma((n,)), dma((n,)), dma((n,)),
+            dma((nz,)), dma((nz,)), dma((plane,)), dma((plane,)), dma, dma, dma,
+            dma((n,)), dma((n,)), dma, dma,
+        ]
+    )
+    vmem = pl.BlockSpec(memory_space=pltpu.VMEM)
+    hbm = pl.BlockSpec(memory_space=pl.ANY)
+    sizes = ((nx, nz, ny), cap, cap_rows, room, chunks)
+    return pl.pallas_call(
+        functools.partial(kernel, sizes),
+        out_shape=(
+            jax.ShapeDtypeStruct((half, width), BF16),
+            jax.ShapeDtypeStruct((8, 128), F32),
+        ),
+        in_specs=[vmem] * 5 + [hbm],
+        out_specs=(hbm, vmem),
+        scratch_shapes=scratch,
+        compiler_params=pltpu.CompilerParams(
+            collective_id=0, has_side_effects=True, vmem_limit_bytes=60 * 1024 * 1024
+        ),
+    )(grad_out.T, combine.T, routes.T, tasks[None], task_lists, gate_up[0].T)
+
+
+def body(*args):
+    fast, flag = fast_body(*args)
+    result = lax.cond(flag[0, 0] > 0.5, lambda a: dense_body(*a), lambda a: fast, args)
+    return result[None]
 
 
 def solution(mesh):

time: 279 us -> 133 us (0.48)
  waiting for transfers between devices: 165 us -> 0 us
  Pallas kernels: 0 us -> 113 us
  starting transfers between devices: 30.3 us -> 0 us
  local copies, waits for them, and re-layouts: 35.8 us -> 5.73 us
  other arithmetic: 18.7 us -> 0 us
  matrix products: 15.2 us -> 0 us
    all_to_all x2 -> x0, waiting for transfers between devices: 130 us -> none  [the longest x1 130 us: body(): lax.all_to_all(send_rows, 'exp', split_axis=0, concat_axis=0, tiled=True)]
    pallas_call x0 -> x1, Pallas kernels: none -> 113 us  [fast_body(): pl.pallas_call(functools.partial(kernel, sizes), out_shape=(jax.ShapeDtyp...]
    reduce_scatter x1 -> x0, waiting for transfers between devices: 34.4 us -> none  [body(): lax.psum_scatter(outer_rows(hidden, masked), 'dp', scatter_dimension=0, t...]
    all_to_all x2 -> x0, starting transfers between devices: 30 us -> none  [the longest x1 16.5 us: body(): lax.all_to_all(send_keep, 'exp', split_axis=0, concat_axis=0, tiled=True)]
    all_to_all x3 -> x0, local copies, waits for them, and re-layouts: 16.6 us -> none  [the longest x2 15.8 us: body(): lax.all_to_all(send_rows, 'exp', split_axis=0, concat_axis=0, tiled=True)]
    dot_general x2 -> x0, matrix products: 15.2 us -> none  [the longest x1 14.4 us: outer_rows(): lax.dot_general(left_rows, right_rows, (((0,), (0,)), ((), ())), preferre...]
    mul x5 -> x0, local copies, waits for them, and re-layouts: 11.7 us -> none  [the longest x3 11.5 us: body(): combine[:, :, None] * grad_out[:, None, :].astype(jnp.float32)]
    scatter x1 -> x0, other arithmetic: 9.63 us -> none  [body(): jnp.zeros((n_experts * capacity, model_width), jnp.bfloat16).at[destination]]
  transfers between devices with their start and end apart: 3 -> 0, of which waited for: 2 -> 0; matrix products, arithmetic and copies ran while one was open for 9% -> 0% of each run, Pallas kernels for 0% -> 0%
where the time goes in v1:
time: 133 us
  Pallas kernels  113 us (85%)
  between operations  14.1 us (11%)
  local copies, waits for them, and re-layouts  5.73 us (4%)
    pallas_call x1, Pallas kernels, fast_body(): pl.pallas_call(functools.partial(kernel, sizes), out_shape=(jax.ShapeDtyp...  113 us
    unnamed x11, local copies, waits for them, and re-layouts  4.54 us

profile of v1, /device:TPU:1, one launch (start us, length us, event | category | flops | bytes accessed | tf_op | source)
XLA Modules:
  0.0 133.2 jit_solution(15673787271250922444)
XLA Ops:
  6.5 0.0 copy-start.3
  6.5 0.0 copy-start.4
  6.5 0.0 copy-start.1
  6.5 0.0 copy-start.2
  6.5 0.0 copy-start
  6.5 113.1 %shard_map.66 = (bf16[720,2880]{1,0:T(8,128)(2,1)}, f32[8,128]{1,0:T(8,128)}) custom-call(bf16[2880,128]{1,0:T(8,128)(2,1)} %bitcast.28, f32[4,128]{1,0:T(4,128)} %bitcast.30, s32[4,128]{1,0:T(4,128)} %bitcast.29, s32[1,128]{1,0:T(1,128)} %bitcast.32, s32[4,64]{1,0:T(4,128)} %lists_ref.1, bf16[2880,768]{1,0:T(8,128)(2,1)} %bitcast.25), custom_call_target="tpu_custom_call" | custom-call | tf_op jit(solution)/shard_map/pallas_call | solution.py:436
  119.7 1.2 slice.15
  121.5 0.0 copy-done.3
  121.5 0.0 copy-done.4
  121.6 0.0 copy-done.1
  121.6 0.0 copy-done.2
  121.6 0.0 copy-done
  121.6 0.3 conditional.1
  121.9 4.5 %copy.37 = bf16[1,720,2880]{2,1,0:T(8,128)(2,1)} copy(bf16[1,720,2880]{2,1,0:T(8,128)(2,1)} %get-tuple-element.33) | data formatting | bytes 8294400
Async XLA Ops:
  6.5 115.0 %copy-start.3 = (s32[4,64]{1,0:T(4,128)S(1)}, s32[4,64]{1,0:T(4,128)}, u32[]{:S(2)}) copy-start(s32[4,64]{1,0:T(4,128)} %lists_ref.1) | copy-start | bytes 3076
  6.5 115.0 %copy-start.4 = (s32[128]{0:T(128)S(1)}, s32[128]{0:T(128)}, u32[]{:S(2)}) copy-start(s32[128]{0:T(128)} %param.11) | copy-start | bytes 1540
  6.5 115.0 %copy-start.1 = (s32[128,4]{0,1:T(4,128)S(1)}, s32[128,4]{0,1:T(4,128)}, u32[]{:S(2)}) copy-start(s32[128,4]{0,1:T(4,128)} %param.10) | copy-start | bytes 6148
  6.5 115.0 %copy-start.2 = (f32[128,4]{0,1:T(4,128)S(1)}, f32[128,4]{0,1:T(4,128)}, u32[]{:S(2)}) copy-start(f32[128,4]{0,1:T(4,128)} %param.9) | copy-start | bytes 6148
  6.5 115.0 %copy-start = (bf16[128,2880]{0,1:T(8,128)(2,1)S(1)}, bf16[128,2880]{0,1:T(8,128)(2,1)}, u32[]{:S(2)}) copy-start(bf16[128,2880]{0,1:T(8,128)(2,1)} %param.8) | copy-start | bytes 2211844

commit v2 on v0

v2 whole, which is shorter than its diff:
```python
import functools

import jax
import jax.numpy as jnp
from jax import lax
from jax.experimental import pallas as pl
from jax.experimental.pallas import tpu as pltpu
from jax.sharding import PartitionSpec as P

F32, BF16, I32 = jnp.float32, jnp.bfloat16, jnp.int32
MESH = pl.DeviceIdType.MESH
GRID = {128: (4, 8, 4), 8: (2, 2, 2)}
CHUNKS = {2880: (256, 256, 384, 384, 384, 384, 384, 256, 192), 320: (128, 128, 64)}
HOPS = {8: (4, 3), 2: (1, 0)}


def iota(shape, dim):
    return lax.broadcasted_iota(I32, shape, dim)


def whole_part(values, step):
    return jnp.floor((values.astype(F32) + 0.5) * (1.0 / step)).astype(I32)


def dot(left, right):
    return jnp.dot(left, right, preferred_element_type=F32)


def dot_lanes(left, right):
    return lax.dot_general(left, right, (((1,), (1,)), ((), ())), preferred_element_type=F32)


def tiles_of(width, step):
    return [(start, min(step, width - start)) for start in range(0, width, step)]


def kernel(
    sizes, tok_ref, comb_ref, routes_ref, task_ref, lists_ref, gate_up_ref, out_ref, *scratch
):
    (nx, nz, ny), cap, cap_rows, chunks = sizes
    n_chunks = len(chunks)
    width, tok_count = tok_ref.shape
    double, slot_rows = gate_up_ref.shape
    hidden_width = double // 2
    half = hidden_width // 2
    experts, plane = nx * nz * ny, nx * ny
    block = nz * cap
    ahead, back = HOPS[nz]

    scratch = list(scratch)
    take = lambda count: [scratch.pop(0) for _ in range(count)]
    tokens, xy_send, xy_recv = (take(n_chunks) for _ in range(3))
    own, dp_send, dp_recv, out_buf = (take(n_chunks) for _ in range(4))
    gu, hidden, spread, weight, meta_send, meta_recv = take(6)
    as_sem, ar_sem, bs_sem, br_sem, xs_sem, xr_sem, xl_sem = take(7)
    ds_sem, dr_sem, out_sem, ms_sem, mr_sem, ml_sem, gu_sem = take(7)

    e_id, p = lax.axis_index("exp"), lax.axis_index("dp")
    y = lax.rem(e_id, ny)
    z = lax.rem(lax.div(e_id, ny), nz)
    x = lax.div(e_id, ny * nz)
    q = x * ny + y
    way = 1 - 2 * p
    z_steps = sorted(range(1, nz), key=lambda d: -min(d, nz - d))
    xy_steps = sorted(
        ((dx, dy) for dx in range(nx) for dy in range(ny) if dx or dy),
        key=lambda s: -(min(s[0], nx - s[0]) + min(s[1], ny - s[1])),
    )

    def along(hops):
        return lax.rem(z + way * hops + 2 * nz, nz)

    def z_at(z2):
        return ((x * nz + z2) * ny + y, p)

    def xy_at(x2, y2):
        return ((x2 * nz + z) * ny + y2, p)

    sibling = (e_id, 1 - p)

    gu_copy = pltpu.make_async_copy(gate_up_ref, gu, gu_sem)
    gu_copy.start()

    barrier = pltpu.get_barrier_semaphore()
    for d in z_steps:
        pl.semaphore_signal(barrier, inc=1, device_id=z_at(lax.rem(z + d, nz)), device_id_type=MESH)
    for dx, dy in xy_steps:
        pl.semaphore_signal(
            barrier, inc=1, device_id=xy_at(lax.rem(x + dx, nx), lax.rem(y + dy, ny)),
            device_id_type=MESH,
        )
    pl.semaphore_signal(barrier, inc=1, device_id=sibling, device_id_type=MESH)

    same = jnp.where(
        iota((tok_count, tok_count), 0) == iota((tok_count, tok_count), 1), 1.0, 0.0
    ).astype(BF16)

    def turn(j):
        start, size = chunks[j]
        tokens[j][z] = dot_lanes(same, tok_ref[start : start + size, :]).astype(BF16)

    def ahead_copy(j, hop):
        slot = along(-hop)
        return pltpu.make_async_remote_copy(
            src_ref=tokens[j].at[slot], dst_ref=tokens[j].at[slot],
            send_sem=as_sem.at[j, hop], recv_sem=ar_sem.at[j, hop],
            device_id=z_at(along(1)), device_id_type=MESH,
        )

    def back_copy(j, hop):
        slot = along(hop)
        return pltpu.make_async_remote_copy(
            src_ref=tokens[j].at[slot], dst_ref=tokens[j].at[slot],
            send_sem=bs_sem.at[j, hop], recv_sem=br_sem.at[j, hop],
            device_id=z_at(along(-1)), device_id_type=MESH,
        )

    def wait_from(ref, sem, device):
        pltpu.make_async_remote_copy(
            src_ref=ref, dst_ref=ref, send_sem=sem, recv_sem=sem,
            device_id=device, device_id_type=MESH,
        ).wait_recv()

    def arrive(j, hop):
        if hop < ahead:
            wait_from(tokens[j].at[along(-hop - 1)], ar_sem.at[j, hop], z_at(along(-1)))
        if hop < back:
            wait_from(tokens[j].at[along(hop + 1)], br_sem.at[j, hop], z_at(along(1)))

    def leave(j, hop):
        if hop < ahead:
            ahead_copy(j, hop).start()
        if hop < back:
            back_copy(j, hop).start()

    def forward(j, hop):
        if j < n_chunks and hop < max(ahead, back):
            arrive(j, hop - 1)
            leave(j, hop)

    def begin(j):
        if j < n_chunks:
            turn(j)
            leave(j, 0)

    turn(0)
    pl.semaphore_wait(barrier, len(z_steps) + len(xy_steps) + 1)
    leave(0, 0)
    begin(1)
    last = max(ahead, back) - 1

    def tick(t):
        for hop in range(last, 0, -1):
            if t >= hop:
                forward(t - hop, hop)
        if t:
            begin(t + 1)

    expert_col = iota((experts, tok_count), 0)
    named = jnp.zeros((experts, tok_count), F32)
    weight_of = jnp.zeros((experts, tok_count), F32)
    for k in range(routes_ref.shape[0]):
        hit = expert_col == routes_ref[k : k + 1, :]
        named = jnp.where(hit, 1.0, named)
        weight_of = jnp.where(hit, comb_ref[k : k + 1, :], weight_of)
    lists = lists_ref[...]
    of_task = iota(lists.shape, 0) == task_ref[0:1, 0:1]
    chosen = jnp.max(jnp.where(of_task, lists, -1), axis=0, keepdims=True)
    trainable = jnp.max(
        jnp.where(iota((experts, lists.shape[1]), 0) == chosen, 1.0, 0.0), axis=1, keepdims=True
    )
    before = jnp.where(
        iota((tok_count, tok_count), 0) < iota((tok_count, tok_count), 1), 1.0, 0.0
    ).astype(BF16)
    slot = dot(named.astype(BF16), before)
    live = named * trainable
    token_row = iota((experts, tok_count), 1).astype(F32) + 1.0
    meta_lane = iota((experts, 128), 1)
    meta = jnp.zeros((experts, 128), F32)
    for c in range(cap):
        here = jnp.where((slot > c - 0.5) & (slot < c + 0.5), live, 0.0)
        at = jnp.sum(here * token_row, axis=1, keepdims=True)
        w = jnp.sum(here * weight_of, axis=1, keepdims=True)
        high = w.astype(BF16).astype(F32)
        mid = (w - high).astype(BF16).astype(F32)
        for kind, value in enumerate((at, high, mid, w - high - mid)):
            meta = jnp.where(meta_lane == kind * cap_rows + c, value, meta)
    meta_send[...] = jnp.transpose(meta)[: 4 * cap_rows, :].astype(BF16)

    def meta_copy(z2):
        return pltpu.make_async_remote_copy(
            src_ref=meta_send, dst_ref=meta_recv.at[z],
            send_sem=ms_sem.at[z2], recv_sem=mr_sem.at[z],
            device_id=z_at(z2), device_id_type=MESH,
        )

    for d in z_steps:
        meta_copy(lax.rem(z + d, nz)).start()
    pltpu.make_async_copy(meta_send, meta_recv.at[z], ml_sem).start()

    step = 96 if hidden_width % 96 == 0 else 32
    pieces = hidden_width // step

    def activate(first, stop):
        @pl.loop(first, stop)
        def _(i):
            rows = pl.ds(pl.multiple_of(i * step, step), step)
            gate = gu[rows, :].astype(F32)
            up = gu[pl.ds(pl.multiple_of(i * step + hidden_width, step), step), :].astype(F32)
            gu[rows, :] = ((up + 1.0) * gate * jax.nn.sigmoid(1.702 * gate)).astype(BF16)

    def reorder():
        for start, size in tiles_of(slot_rows, 256):
            to = iota((slot_rows, size), 1) + start
            to_q = whole_part(to, block)
            rest = to - to_q * block
            to_z = whole_part(rest, cap)
            c = rest - to_z * cap
            to_x = whole_part(to_q, ny)
            source = ((to_x * nz + to_z) * ny + (to_q - to_x * ny)) * cap + c
            order = jnp.where(iota((slot_rows, size), 0) == source, 1.0, 0.0).astype(BF16)
            hidden[:, start : start + size] = dot(gu[0:hidden_width, :], order).astype(BF16)

    def place_slots():
        for d in z_steps:
            z2 = lax.rem(z + nz - d, nz)
            wait_from(meta_recv.at[z2], mr_sem.at[z2], z_at(z2))
        pltpu.make_async_copy(meta_send, meta_recv.at[z], ml_sem).wait()
        s_q = whole_part(iota((slot_rows, experts), 0), block)
        s_x = whole_part(s_q, ny)
        expert_of = (s_x * nz + z) * ny + (s_q - s_x * ny)
        at_expert = jnp.where(expert_of == iota((slot_rows, experts), 1), 1.0, 0.0).astype(BF16)
        m_col = iota((slot_rows, cap_rows * 4), 0)
        m_lane = iota((slot_rows, cap_rows * 4), 1)
        m_rest = m_col - whole_part(m_col, block) * block
        m_z = whole_part(m_rest, cap)
        m_c = m_rest - m_z * cap
        totals = jnp.zeros((slot_rows, cap_rows * 4), F32)
        for z2 in range(nz):
            totals = jnp.where(m_z == z2, dot_lanes(at_expert, meta_recv[z2]), totals)
        kind_of = whole_part(m_lane, cap_rows)
        slot_hit = m_lane - kind_of * cap_rows == m_c
        at = jnp.sum(jnp.where(slot_hit & (kind_of == 0), totals, 0.0), axis=1, keepdims=True)
        w = jnp.sum(jnp.where(slot_hit & (kind_of > 0), totals, 0.0), axis=1, keepdims=True)
        weight[...] = jnp.broadcast_to(w, weight.shape)
        r_col = iota((slot_rows, 1), 0)
        r_rest = r_col - whole_part(r_col, block) * block
        at = jnp.where(at > 0.5, at - 1.0 + (whole_part(r_rest, cap) * tok_count).astype(F32), -1.0)
        spread[...] = jnp.where(
            iota((slot_rows, nz * tok_count), 1).astype(F32) == at, 1.0, 0.0
        ).astype(BF16)

    def xy_copy(j, x2, y2):
        q2 = x2 * ny + y2
        return pltpu.make_async_remote_copy(
            src_ref=xy_send[j].at[q2], dst_ref=xy_recv[j].at[q],
            send_sem=xs_sem.at[j, q2], recv_sem=xr_sem.at[j, q],
            device_id=xy_at(x2, y2), device_id_type=MESH,
        )

    def dp_copy(j):
        return pltpu.make_async_remote_copy(
            src_ref=dp_send[j], dst_ref=dp_recv[j], send_sem=ds_sem.at[j], recv_sem=dr_sem.at[j],
            device_id=sibling, device_id_type=MESH,
        )

    def each_xy(act):
        for dx, dy in xy_steps:
            act(lax.rem(x + dx, nx), lax.rem(y + dy, ny))

    def send_xy(j):
        arrive(j, last)
        for start, part in tiles_of(chunks[j][1], 256):
            rows = tokens[j][:, :, start : start + part].reshape(nz * tok_count, part)
            by = jnp.concatenate([weight[...]] * 2, axis=1)[:, :part]
            xy_send[j][:, :, start : start + part] = (
                (dot(spread[...], rows) * by).astype(BF16).reshape(plane, block, part)
            )
        each_xy(lambda x2, y2: xy_copy(j, x2, y2).start())
        pltpu.make_async_copy(xy_send[j].at[q], xy_recv[j].at[q], xl_sem.at[j]).start()

    def multiply(j):
        def arrived(x2, y2):
            q2 = x2 * ny + y2
            wait_from(xy_recv[j].at[q2], xr_sem.at[j, q2], xy_at(x2, y2))

        each_xy(arrived)
        pltpu.make_async_copy(xy_send[j].at[q], xy_recv[j].at[q], xl_sem.at[j]).wait()
        theirs = pl.ds(pl.multiple_of((1 - p) * half, 16), half)
        mine = pl.ds(pl.multiple_of(p * half, 16), half)
        parts = tiles_of(chunks[j][1], 256)
        for start, part in parts:
            rows = xy_recv[j][:, :, start : start + part].reshape(slot_rows, part)
            dp_send[j][:, start : start + part] = dot(hidden[theirs, :], rows).astype(BF16)
        dp_copy(j).start()
        for start, part in parts:
            rows = xy_recv[j][:, :, start : start + part].reshape(slot_rows, part)
            own[j][:, start : start + part] = dot(hidden[mine, :], rows)

    def out_copy(j):
        start, size = chunks[j]
        return pltpu.make_async_copy(
            out_buf[j], out_ref.at[:, start : start + size], out_sem.at[j]
        )

    def finish(j):
        dp_copy(j).wait_recv()
        out_buf[j][...] = (own[j][...] + dp_recv[j][...].astype(F32)).astype(BF16)
        out_copy(j).start()

    third = pieces // 3
    duties = {
        1: [gu_copy.wait, lambda: activate(0, third)],
        2: [lambda: activate(third, 2 * third)],
        3: [place_slots],
        4: [lambda: activate(2 * third, pieces), reorder],
    }
    for t in range(n_chunks + last + 3):
        if t:
            tick(t)
        for when in sorted(duties):
            if when == t or (last < 3 and t == 0):
                for duty in duties[when]:
                    duty()
        if 0 <= t - last - 2 < n_chunks:
            multiply(t - last - 2)
        if 0 <= t - last < n_chunks:
            send_xy(t - last)
        if 0 <= t - last - 3:
            finish(t - last - 3)

    for d in z_steps:
        meta_copy(lax.rem(z + d, nz)).wait_send()
    for j in range(n_chunks):
        for hop in range(ahead):
            ahead_copy(j, hop).wait_send()
        for hop in range(back):
            back_copy(j, hop).wait_send()
        each_xy(lambda x2, y2: xy_copy(j, x2, y2).wait_send())
        dp_copy(j).wait_send()
        out_copy(j).wait()


def body(grad_out, combine, routes, tasks, task_lists, gate_up):
    n_experts = lax.axis_size("exp")
    nx, nz, ny = GRID[n_experts]
    slot_rows = gate_up.shape[1]
    cap = slot_rows // n_experts
    cap_rows = -(-cap // 8) * 8
    tok_count, width = grad_out.shape
    starts = [sum(CHUNKS[width][:i]) for i in range(len(CHUNKS[width]))]
    chunks = list(zip(starts, CHUNKS[width]))
    hidden_width = gate_up.shape[2] // 2
    half = hidden_width // 2
    plane, block = nx * ny, nz * cap
    n = len(chunks)
    ahead, back = HOPS[nz]
    dma = pltpu.SemaphoreType.DMA
    each = lambda shape, kind: [pltpu.VMEM((*shape, size), kind) for _, size in chunks]
    meta = (4 * cap_rows, n_experts)
    scratch = (
        each((nz, tok_count), BF16)
        + each((plane, block), BF16) + each((plane, block), BF16)
        + each((half,), F32) + each((half,), BF16) + each((half,), BF16) + each((half,), BF16)
        + [
            pltpu.VMEM((2 * hidden_width, slot_rows), BF16),
            pltpu.VMEM((hidden_width, slot_rows), BF16),
            pltpu.VMEM((slot_rows, nz * tok_count), BF16),
            pltpu.VMEM((slot_rows, 128), F32),
            pltpu.VMEM(meta, BF16), pltpu.VMEM((nz, *meta), BF16),
            dma((n, ahead)), dma((n, ahead)), dma((n, max(back, 1))), dma((n, max(back, 1))),
            dma((n, plane)), dma((n, plane)), dma((n,)),
            dma((n,)), dma((n,)), dma((n,)), dma((nz,)), dma((nz,)), dma, dma,
        ]
    )
    vmem = pl.BlockSpec(memory_space=pltpu.VMEM)
    hbm = pl.BlockSpec(memory_space=pl.ANY)
    sizes = ((nx, nz, ny), cap, cap_rows, chunks)
    return pl.pallas_call(
        functools.partial(kernel, sizes),
        out_shape=jax.ShapeDtypeStruct((half, width), BF16),
        in_specs=[vmem] * 5 + [hbm],
        out_specs=hbm,
        scratch_shapes=scratch,
        compiler_params=pltpu.CompilerParams(
            collective_id=0, has_side_effects=True, vmem_limit_bytes=60 * 1024 * 1024
        ),
    )(grad_out.T, combine.T, routes.T, tasks[None], task_lists, gate_up[0].T)[None]


def solution(mesh):
    in_specs = (
        P(("exp", "dp"), None),
        P(("exp", "dp"), None),
        P(("exp", "dp"), None),
        P(("exp", "dp")),
        P(),
        P("exp", "dp", None),
    )
    out_specs = P("exp", "dp", None)
    return jax.shard_map(body, mesh=mesh, in_specs=in_specs, out_specs=out_specs, check_vma=False)
```

time: 279 us -> 101 us (0.36)
  waiting for transfers between devices: 165 us -> 0 us
  Pallas kernels: 0 us -> 96.6 us
  local copies, waits for them, and re-layouts: 35.8 us -> 4.52 us
  starting transfers between devices: 30.3 us -> 0 us
  other arithmetic: 18.7 us -> 0 us
  matrix products: 15.2 us -> 0 us
  between operations: 13.5 us -> 0.01 us
    all_to_all x2 -> x0, waiting for transfers between devices: 130 us -> none  [the longest x1 130 us: body(): lax.all_to_all(send_rows, 'exp', split_axis=0, concat_axis=0, tiled=True)]
    pallas_call x0 -> x1, Pallas kernels: none -> 96.6 us  [body(): pl.pallas_call(functools.partial(kernel, sizes), out_shape=jax.ShapeDtype...]
    reduce_scatter x1 -> x0, waiting for transfers between devices: 34.4 us -> none  [body(): lax.psum_scatter(outer_rows(hidden, masked), 'dp', scatter_dimension=0, t...]
    all_to_all x2 -> x0, starting transfers between devices: 30 us -> none  [the longest x1 16.5 us: body(): lax.all_to_all(send_keep, 'exp', split_axis=0, concat_axis=0, tiled=True)]
    all_to_all x3 -> x0, local copies, waits for them, and re-layouts: 16.6 us -> none  [the longest x2 15.8 us: body(): lax.all_to_all(send_rows, 'exp', split_axis=0, concat_axis=0, tiled=True)]
    dot_general x2 -> x0, matrix products: 15.2 us -> none  [the longest x1 14.4 us: outer_rows(): lax.dot_general(left_rows, right_rows, (((0,), (0,)), ((), ())), preferre...]
    mul x5 -> x0, local copies, waits for them, and re-layouts: 11.7 us -> none  [the longest x3 11.5 us: body(): combine[:, :, None] * grad_out[:, None, :].astype(jnp.float32)]
    scatter x1 -> x0, other arithmetic: 9.63 us -> none  [body(): jnp.zeros((n_experts * capacity, model_width), jnp.bfloat16).at[destination]]
  transfers between devices with their start and end apart: 3 -> 0, of which waited for: 2 -> 0; matrix products, arithmetic and copies ran while one was open for 9% -> 0% of each run, Pallas kernels for 0% -> 0%
where the time goes in v2:
time: 101 us
  Pallas kernels  96.6 us (96%)
  local copies, waits for them, and re-layouts  4.52 us (4%)
    pallas_call x1, Pallas kernels, body(): pl.pallas_call(functools.partial(kernel, sizes), out_shape=jax.ShapeDtype...  96.6 us
    unnamed x1, local copies, waits for them, and re-layouts  4.52 us

profile of v2, /device:TPU:1, one launch (start us, length us, event | category | flops | bytes accessed | tf_op | source)
XLA Modules:
  0.0 101.2 jit_solution(13682156623349184737)
XLA Ops:
  0.0 96.6 %shard_map.64 = bf16[720,2880]{1,0:T(8,128)(2,1)} custom-call(bf16[2880,128]{1,0:T(8,128)(2,1)} %bitcast.10, f32[4,128]{1,0:T(4,128)} %bitcast.11, s32[4,128]{1,0:T(4,128)} %bitcast.12, s32[1,128]{1,0:T(1,128)} %bitcast.13, s32[4,64]{1,0:T(4,128)} %lists_ref.1, bf16[2880,768]{1,0:T(8,128)(2,1)} %bitcast.9), custom_call_target="tpu_custom_call" | custom-call | tf_op jit(solution)/shard_map/pallas_call | solution.py:379
  96.6 4.5 %copy.8 = bf16[1,720,2880]{2,1,0:T(8,128)(2,1)} copy(bf16[1,720,2880]{2,1,0:T(8,128)(2,1)} %bitcast.8) | data formatting | bytes 8294400

commit v3 on v2

--- a/solution.py
+++ b/solution.py
@@ -315,19 +315,19 @@
         3: [place_slots],
         4: [lambda: activate(2 * third, pieces), reorder],
     }
-    for t in range(n_chunks + last + 3):
+    for t in range(n_chunks + last + 4):
         if t:
             tick(t)
         for when in sorted(duties):
             if when == t or (last < 3 and t == 0):
                 for duty in duties[when]:
                     duty()
-        if 0 <= t - last - 2 < n_chunks:
-            multiply(t - last - 2)
+        if 0 <= t - last - 3 < n_chunks:
+            multiply(t - last - 3)
         if 0 <= t - last < n_chunks:
             send_xy(t - last)
-        if 0 <= t - last - 3:
-            finish(t - last - 3)
+        if 0 <= t - last - 4:
+            finish(t - last - 4)
 
     for d in z_steps:
         meta_copy(lax.rem(z + d, nz)).wait_send()
@@ -339,6 +339,20 @@
         each_xy(lambda x2, y2: xy_copy(j, x2, y2).wait_send())
         dp_copy(j).wait_send()
         out_copy(j).wait()
+
+
+def hand_over(held_ref, out_ref, pieces, in_sems, out_sems):
+    rows = pieces.shape[1]
+    parts = [pl.ds(i * rows, rows) for i in range(pieces.shape[0])]
+    ins = [pltpu.make_async_copy(held_ref.at[r], pieces.at[i], in_sems.at[i]) for i, r in enumerate(parts)]
+    outs = [pltpu.make_async_copy(pieces.at[i], out_ref.at[r], out_sems.at[i]) for i, r in enumerate(parts)]
+    for copy in ins:
+        copy.start()
+    for copy, then in zip(ins, outs):
+        copy.wait()
+        then.start()
+    for copy in outs:
+        copy.wait()
 
 
 def body(grad_out, combine, routes, tasks, task_lists, gate_up):
@@ -376,7 +390,7 @@
     vmem = pl.BlockSpec(memory_space=pltpu.VMEM)
     hbm = pl.BlockSpec(memory_space=pl.ANY)
     sizes = ((nx, nz, ny), cap, cap_rows, chunks)
-    return pl.pallas_call(
+    result = pl.pallas_call(
         functools.partial(kernel, sizes),
         out_shape=jax.ShapeDtypeStruct((half, width), BF16),
         in_specs=[vmem] * 5 + [hbm],
@@ -385,7 +399,16 @@
         compiler_params=pltpu.CompilerParams(
             collective_id=0, has_side_effects=True, vmem_limit_bytes=60 * 1024 * 1024
         ),
-    )(grad_out.T, combine.T, routes.T, tasks[None], task_lists, gate_up[0].T)[None]
+    )(grad_out.T, combine.T, routes.T, tasks[None], task_lists, gate_up[0].T)
+    parts = 9 if half % 144 == 0 else 1
+    return pl.pallas_call(
+        hand_over,
+        out_shape=jax.ShapeDtypeStruct((half, width), BF16),
+        in_specs=[hbm],
+        out_specs=hbm,
+        scratch_shapes=[pltpu.VMEM((parts, half // parts, width), BF16), dma((parts,)), dma((parts,))],
+        compiler_params=pltpu.CompilerParams(vmem_limit_bytes=60 * 1024 * 1024),
+    )(result)[None]
 
 
 def solution(mesh):

time: 101 us -> 97.5 us (0.965)
  local copies, waits for them, and re-layouts: 4.52 us -> 0 us
    unnamed x1 -> x0, local copies, waits for them, and re-layouts: 4.52 us -> none
    pallas_call x0 -> x1, Pallas kernels: none -> 3.68 us  [body(): pl.pallas_call(hand_over, out_shape=jax.ShapeDtypeStruct((half, width), B...]
    pallas_call x1, Pallas kernels: 96.6 us -> 93.5 us  [body(): pl.pallas_call(functools.partial(kernel, sizes), out_shape=jax.ShapeDtype...]
where the time goes in v3:
time: 97.5 us; the launch traced here: 97.4 us
  Pallas kernels  97.2 us (100%)
    pallas_call x1, Pallas kernels, body(): pl.pallas_call(functools.partial(kernel, sizes), out_shape=jax.ShapeDtype...  93.5 us
    pallas_call x1, Pallas kernels, body(): pl.pallas_call(hand_over, out_shape=jax.ShapeDtypeStruct((half, width), B...  3.68 us

profile of v3, /device:TPU:1, one launch (start us, length us, event | category | flops | bytes accessed | tf_op | source)
XLA Modules:
  0.0 97.4 jit_solution(8535635927184396594)
XLA Ops:
  0.0 93.5 %shard_map.64.held_ref = bf16[720,2880]{1,0:T(8,128)(2,1)} custom-call(bf16[2880,128]{1,0:T(8,128)(2,1)} %bitcast.9, f32[4,128]{1,0:T(4,128)} %bitcast.10, s32[4,128]{1,0:T(4,128)} %bitcast.11, s32[1,128]{1,0:T(1,128)} %bitcast.12, s32[4,64]{1,0:T(4,128)} %lists_ref.1, bf16[2880,768]{1,0:T(8,128)(2,1)} %bitcast.8), custom_call_target="tpu_custom_call" | custom-call | tf_op jit(solution)/shard_map/pallas_call | solution.py:393
  93.5 3.7 %shard_map.65 = bf16[720,2880]{1,0:T(8,128)(2,1)} custom-call(bf16[720,2880]{1,0:T(8,128)(2,1)} %shard_map.64.held_ref), custom_call_target="tpu_custom_call" | custom-call | tf_op jit(solution)/shard_map/pallas_call | solution.py:404

commit v4 on v3

--- a/solution.py
+++ b/solution.py
@@ -121,31 +121,38 @@
             device_id=device, device_id_type=MESH,
         ).wait_recv()
 
-    def arrive(j, hop):
-        if hop < ahead:
-            wait_from(tokens[j].at[along(-hop - 1)], ar_sem.at[j, hop], z_at(along(-1)))
-        if hop < back:
-            wait_from(tokens[j].at[along(hop + 1)], br_sem.at[j, hop], z_at(along(1)))
-
-    def leave(j, hop):
-        if hop < ahead:
+    def ahead_in(j, hop):
+        wait_from(tokens[j].at[along(-hop - 1)], ar_sem.at[j, hop], z_at(along(-1)))
+
+    def back_in(j, hop):
+        wait_from(tokens[j].at[along(hop + 1)], br_sem.at[j, hop], z_at(along(1)))
+
+    def forward(j, hop):
+        if j < n_chunks and hop < ahead:
+            ahead_in(j, hop - 1)
             ahead_copy(j, hop).start()
-        if hop < back:
+        if j < n_chunks and hop < back:
+            back_in(j, hop - 1)
             back_copy(j, hop).start()
 
-    def forward(j, hop):
-        if j < n_chunks and hop < max(ahead, back):
-            arrive(j, hop - 1)
-            leave(j, hop)
+    def arrive(j):
+        if back:
+            back_in(j, back - 1)
+        ahead_in(j, ahead - 1)
+
+    def leave(j):
+        ahead_copy(j, 0).start()
+        if back:
+            back_copy(j, 0).start()
 
     def begin(j):
         if j < n_chunks:
             turn(j)
-            leave(j, 0)
+            leave(j)
 
     turn(0)
     pl.semaphore_wait(barrier, len(z_steps) + len(xy_steps) + 1)
-    leave(0, 0)
+    leave(0)
     begin(1)
     last = max(ahead, back) - 1
 
@@ -269,7 +276,7 @@
             act(lax.rem(x + dx, nx), lax.rem(y + dy, ny))
 
     def send_xy(j):
-        arrive(j, last)
+        arrive(j)
         for start, part in tiles_of(chunks[j][1], 256):
             rows = tokens[j][:, :, start : start + part].reshape(nz * tok_count, part)
             by = jnp.concatenate([weight[...]] * 2, axis=1)[:, :part]
@@ -311,9 +318,10 @@
     third = pieces // 3
     duties = {
         1: [gu_copy.wait, lambda: activate(0, third)],
-        2: [lambda: activate(third, 2 * third)],
-        3: [place_slots],
-        4: [lambda: activate(2 * third, pieces), reorder],
+        2: [place_slots],
+        3: [],
+        4: [lambda: activate(third, 2 * third)],
+        5: [lambda: activate(2 * third, pieces), reorder],
     }
     for t in range(n_chunks + last + 4):
         if t:
@@ -322,12 +330,12 @@
             if when == t or (last < 3 and t == 0):
                 for duty in duties[when]:
                     duty()
+        if 0 <= t - last - 4:
+            finish(t - last - 4)
         if 0 <= t - last - 3 < n_chunks:
             multiply(t - last - 3)
         if 0 <= t - last < n_chunks:
             send_xy(t - last)
-        if 0 <= t - last - 4:
-            finish(t - last - 4)
 
     for d in z_steps:
         meta_copy(lax.rem(z + d, nz)).wait_send()

time: 97.5 us -> 97.5 us (level)
  no operation moved by 1% of the time
where the time goes in v4:
time: 97.5 us; the launch traced here: 97 us
  Pallas kernels  96.9 us (99%)
    pallas_call x1, Pallas kernels, body(): pl.pallas_call(functools.partial(kernel, sizes), out_shape=jax.ShapeDtype...  93.2 us
    pallas_call x1, Pallas kernels, body(): pl.pallas_call(hand_over, out_shape=jax.ShapeDtypeStruct((half, width), B...  3.68 us

profile of v4, /device:TPU:1, one launch (start us, length us, event | category | flops | bytes accessed | tf_op | source)
XLA Modules:
  0.0 97.0 jit_solution(15440731151616422184)
XLA Ops:
  0.0 93.2 %shard_map.64.held_ref = bf16[720,2880]{1,0:T(8,128)(2,1)} custom-call(bf16[2880,128]{1,0:T(8,128)(2,1)} %bitcast.9, f32[4,128]{1,0:T(4,128)} %bitcast.10, s32[4,128]{1,0:T(4,128)} %bitcast.11, s32[1,128]{1,0:T(1,128)} %bitcast.12, s32[4,64]{1,0:T(4,128)} %lists_ref.1, bf16[2880,768]{1,0:T(8,128)(2,1)} %bitcast.8), custom_call_target="tpu_custom_call" | custom-call | tf_op jit(solution)/shard_map/pallas_call | solution.py:401
  93.2 3.7 %shard_map.65 = bf16[720,2880]{1,0:T(8,128)(2,1)} custom-call(bf16[720,2880]{1,0:T(8,128)(2,1)} %shard_map.64.held_ref), custom_call_target="tpu_custom_call" | custom-call | tf_op jit(solution)/shard_map/pallas_call | solution.py:412
